TPU v7x, 32 devices: a whole 2x2x4 slice. The times are simulated.
32 devices in a mesh: section: 2 (over core), dom: 16 (over z, y, x).
Axes of the slice: x: 2, y: 2, z: 4, core: 2. Of those that a mesh axis runs over, the one named last changes fastest.
Arguments:
- node_feats: bfloat16 [2, 4096, 512], P(None, 'dom'), may hold values from -6 to 6
- edge_feats: bfloat16 [2, 8192, 512], P(None, 'dom'), may hold values from -6 to 6
- edge_src: int32 [8192], P('dom'), may hold values from 0 to 287, as said below
- edge_dst: int32 [8192], P('dom'), may hold values from 0 to 255
- edge_count: int32 [16], P('dom'), may hold values from 256 to 512, as said below
- send_rows: int32 [256, 2], P('dom'), may hold values from 0 to 255
- edge_w1: bfloat16 [2, 3, 512, 512], P('section'), may hold values from -0.15625 to 0.15625
- edge_b1: bfloat16 [2, 512], P('section'), may hold values from -3 to 3
- edge_w2: bfloat16 [2, 512, 512], P('section'), may hold values from -0.25 to 0.25
- edge_gain: bfloat16 [2, 512], P('section'), may hold values from 0.5 to 1.5
- node_w1: bfloat16 [2, 2, 512, 512], P('section'), may hold values from -0.1875 to 0.1875
- node_b1: bfloat16 [2, 512], P('section'), may hold values from -3 to 3
- node_w2: bfloat16 [2, 512, 512], P('section'), may hold values from -0.25 to 0.25
- node_gain: bfloat16 [2, 512], P('section'), may hold values from 0.5 to 1.5
Outputs:
- node_out: bfloat16 [2, 2, 4096, 512], P('section', None, 'dom')
- edge_out: bfloat16 [2, 2, 8192, 512], P('section', None, 'dom')
Inputs may be any that keep to these rules, and one draw needn't show every extreme that they name: `edge_src`: among a device's 512 slots, the first 32 name each value from 256 upward exactly once; the others are below 256. `edge_count`: some device has all 512 slots live.
All inputs are finite; a program needn't handle non-finite values.
Results may differ from a plain program's by a relative error of at most 0.0065.
Values may be sent and summed in bfloat16 or wider, within the bound.
A program may use at most 64 MiB of HBM per device.

v0:
```python
import jax
import jax.numpy as jnp
from jax import lax
from jax.sharding import PartitionSpec as P


def from_behind(block, axis, distance):
    devices = range(lax.axis_size(axis))
    route = [(i - distance, i) for i in devices if i - distance in devices]
    return lax.ppermute(block, axis, route)


def project(values, weight):
    return jnp.dot(values, weight, preferred_element_type=jnp.float32)


def layer_norm(values, gain):
    row_mean = jnp.mean(values, axis=-1, keepdims=True)
    centred = values - row_mean
    row_var = jnp.mean(centred * centred, axis=-1, keepdims=True)
    return centred * lax.rsqrt(row_var + 1e-05) * gain.astype(jnp.float32)


def apply_layer(node_lat, edge_lat, weights, graph_info):
    edge_w1, edge_b1, edge_w2, edge_gain, node_w1, node_b1, node_w2, node_gain = weights
    edge_src, edge_dst, live_mask, send_rows = graph_info
    outgoing = jnp.take(node_lat, send_rows, axis=0)
    arrived = lax.all_to_all(outgoing, "dom", split_axis=0, concat_axis=0, tiled=True)
    extended = jnp.concatenate([node_lat, arrived.reshape(-1, node_lat.shape[1])], axis=0)
    from_sender = project(extended, edge_w1[1])
    from_receiver = project(node_lat, edge_w1[2])
    hidden = project(edge_lat, edge_w1[0]) + jnp.take(from_sender, edge_src, axis=0)
    hidden = hidden + jnp.take(from_receiver, edge_dst, axis=0) + edge_b1.astype(jnp.float32)
    hidden = jax.nn.silu(hidden).astype(jnp.bfloat16)
    update = layer_norm(project(hidden, edge_w2), edge_gain) * live_mask[:, None]
    message = update.astype(jnp.bfloat16)
    new_edges = (edge_lat.astype(jnp.float32) + update).astype(jnp.bfloat16)
    node_ids = lax.broadcasted_iota(jnp.int32, (node_lat.shape[0], edge_lat.shape[0]), 0)
    onehot = (node_ids == edge_dst[None, :]).astype(jnp.bfloat16)
    incoming = project(onehot, message).astype(jnp.bfloat16)
    node_hidden = (
        project(node_lat, node_w1[0]) + project(incoming, node_w1[1]) + node_b1.astype(jnp.float32)
    )
    node_hidden = jax.nn.silu(node_hidden).astype(jnp.bfloat16)
    node_update = layer_norm(project(node_hidden, node_w2), node_gain)
    new_nodes = (node_lat.astype(jnp.float32) + node_update).astype(jnp.bfloat16)
    return (new_nodes, new_edges)


def local(
    node_feats,
    edge_feats,
    edge_src,
    edge_dst,
    edge_count,
    send_rows,
    edge_w1,
    edge_b1,
    edge_w2,
    edge_gain,
    node_w1,
    node_b1,
    node_w2,
    node_gain,
):
    batches = node_feats.shape[0]
    node_count = node_feats.shape[1]
    edge_slots = edge_feats.shape[1]
    width = node_feats.shape[2]
    section_idx = lax.axis_index("section")
    sections = lax.axis_size("section")
    positions = lax.broadcasted_iota(jnp.int32, (edge_slots,), 0)
    live_mask = (positions < edge_count[0]).astype(jnp.float32)
    graph_info = (edge_src, edge_dst, live_mask, send_rows)
    own_weights = (
        edge_w1[0],
        edge_b1[0],
        edge_w2[0],
        edge_gain[0],
        node_w1[0],
        node_b1[0],
        node_w2[0],
        node_gain[0],
    )
    received = jnp.zeros((node_count + edge_slots, width), jnp.bfloat16)
    results = [received for batch_num in range(batches)]
    ticks = batches + sections - 1
    for tick_num in range(ticks):
        pick = min(tick_num, batches - 1)
        fresh_input = jnp.concatenate([node_feats[pick], edge_feats[pick]], axis=0)
        current = jnp.where(section_idx == 0, fresh_input, received)
        new_nodes, new_edges = apply_layer(
            current[:node_count], current[node_count:], own_weights, graph_info
        )
        combined = jnp.concatenate([new_nodes, new_edges], axis=0)
        for batch_num in range(batches):
            results[batch_num] = jnp.where(
                tick_num - section_idx == batch_num, combined, results[batch_num]
            )
        if tick_num + 1 < ticks:
            received = from_behind(combined, "section", 1)
    stacked = jnp.stack(results)[None]
    return (stacked[:, :, :node_count], stacked[:, :, node_count:])


def solution(mesh):
    in_specs = (
        P(None, "dom", None),
        P(None, "dom", None),
        P("dom"),
        P("dom"),
        P("dom"),
        P("dom", None),
        P("section", None, None, None),
        P("section", None),
        P("section", None, None),
        P("section", None),
        P("section", None, None, None),
        P("section", None),
        P("section", None, None),
        P("section", None),
    )
    out_specs = (P("section", None, "dom", None), P("section", None, "dom", None))
    return jax.shard_map(local, mesh=mesh, in_specs=in_specs, out_specs=out_specs, check_vma=False)
```

profile of v0, /device:TPU:1, one launch (start us, length us, event | category | flops | bytes accessed | tf_op | source)
XLA Modules:
  0.0 109.2 jit_solution(17650106743988087679)
XLA Ops:
  2.1 2.1 %slice_bitcast_fusion.1 = (bf16[512,512]{1,0:T(8,128)(2,1)}, bf16[512,512]{1,0:T(8,128)(2,1)S(1)}) fusion(bf16[2,512,512]{2,1,0:T(8,128)(2,1)} %param.21), kind=kLoop, calls=%fused_computation.123 | loop fusion | bytes 2097152 | tf_op jit(solution)/shard_map/squeeze | solution.py:90
  7.9 7.4 %all-to-all-start = ((bf16[16,2,512]{2,1,0:T(2,128)(2,1)}), bf16[16,2,512]{2,1,0:T(2,128)(2,1)S(1)}, u32[]{:S(2)}, u32[]{:S(2)}) async-start(bf16[16,2,512]{2,1,0:T(2,128)(2,1)} %broadcast_select_fusion.4), calls=%async_computation | async-start | bytes 65536 | tf_op jit(solution)/shard_map/all_to_all | solution.py:28
  15.8 2.1 %fusion.56 = f32[256,512]{1,0:T(8,128)} fusion(bf16[1,2,512,512]{3,2,1,0:T(8,128)(2,1)} %param.30, bf16[768,512]{1,0:T(8,128)(2,1)S(1)} %maximum_select_fusion), kind=kOutput, calls=%fused_computation.89 | convolution fusion | flops 134217728 | bytes 1310720 | tf_op jit(solution)/shard_map/dot_general | solution.py:14
  18.7 2.3 %gather_fusion.2 = f32[512,512]{1,0:T(8,128)} fusion(f32[256,512]{1,0:T(8,128)S(1)} %fusion.40, s32[1024]{0:T(1024)S(1)} %pad_clamp_fusion), kind=kCustom, calls=%fused_computation.2.clone | custom fusion | bytes 2099200 | tf_op jit(solution)/shard_map/jit(_take)/gather | solution.py:33
  22.9 2.3 %gather_fusion.1 = f32[512,512]{1,0:T(8,128)} fusion(f32[288,512]{1,0:T(8,128)S(1)} %fusion.46, s32[1024]{0:T(1024)S(1)} %pad_clamp_fusion.1), kind=kCustom, calls=%fused_computation.1.clone | custom fusion | bytes 2099200 | tf_op jit(solution)/shard_map/jit(_take)/gather | solution.py:32
  25.2 3.4 %fusion.175 = (f32[512]{0:T(512)S(1)}, f32[512,512]{1,0:T(8,128)}) fusion(bf16[1,512,512]{2,1,0:T(8,128)(2,1)S(1)} %copy-done, f32[512,512]{1,0:T(8,128)} %gather_fusion.2, f32[512,512]{1,0:T(8,128)} %gather_fusion.1, f32[512]{0:T(512)S(1)} %bitcast.125, pred[512]{0:T(512)(128)(4,1)S(1)} %get-tuple-element.23, pred[512]{0:T(512)(128)(4,1)S(1)} %get-tuple-element.24, ...), kind=kOutput, calls=%fused_computation.210 | convolution fusion | flops 539753984 | bytes 4723712 | tf_op jit(solution)/shard_map/dot_general | solution.py:14
  28.7 1.6 %multiply_reduce_fusion.2 = f32[512]{0:T(512)S(1)} fusion(f32[512,512]{1,0:T(8,128)} %get-tuple-element.12, f32[512]{0:T(512)S(1)} %broadcast_multiply_fusion.2), kind=kLoop, calls=%fused_computation.40 | loop fusion | flops 785920 | bytes 1052672 | tf_op jit(solution)/shard_map/reduce_sum | solution.py:20
  30.6 3.2 %multiply_convert_fusion.5 = bf16[256,512]{1,0:T(8,128)(2,1)} fusion(f32[256,512]{1,0:T(8,128)} %fusion.56, f32[512,512]{1,0:T(8,128)} %get-tuple-element.12, f32[512]{0:T(512)S(1)} %fusion.155, f32[512]{0:T(512)S(1)} %bitcast.117, f32[512]{0:T(512)S(1)} %add_rsqrt_fusion.2, f32[512]{0:T(512)S(1)} %broadcast_multiply_fusion.2, ...), kind=kOutput, calls=%fused_computation.106 | convolution fusion | flops 270925824 | bytes 2371584 | tf_op jit(solution)/shard_map/dot_general | solution.py:14
  33.8 1.5 %fusion.180 = (f32[256]{0:T(256)S(1)}, f32[256,512]{1,0:T(8,128)S(1)}) fusion(bf16[256,512]{1,0:T(8,128)(2,1)} %multiply_convert_fusion.5, bf16[1,512,512]{2,1,0:T(8,128)(2,1)} %param.32), kind=kOutput, calls=%fused_computation.211 | convolution fusion | flops 134348544 | bytes 1311744 | tf_op jit(solution)/shard_map/dot_general | solution.py:14
  35.8 1.3 %collective-permute-start = (bf16[768,512]{1,0:T(8,128)(2,1)S(1)}, bf16[768,512]{1,0:T(8,128)(2,1)S(1)}, u32[]{:S(2)}, u32[]{:S(2)}) collective-permute-start(bf16[768,512]{1,0:T(8,128)(2,1)S(1)} %pad_maximum_fusion.1), channel_id=1, source_target_pairs={{0,16},{1,17},{2,18},{3,19},{4,20},{5,21},{6,22},{7,23},{8,24},{9,... | collective-permute-start | bytes 2359304 | tf_op jit(solution)/shard_map/ppermute | solution.py:10
  37.1 3.9 %collective-permute-done = bf16[768,512]{1,0:T(8,128)(2,1)S(1)} collective-permute-done((bf16[768,512]{1,0:T(8,128)(2,1)S(1)}, bf16[768,512]{1,0:T(8,128)(2,1)S(1)}, u32[]{:S(2)}, u32[]{:S(2)}) %collective-permute-start) | collective-permute-done | bytes 786464 | tf_op jit(solution)/shard_map/ppermute | solution.py:10
  42.6 4.9 %all-to-all-start.1 = ((bf16[16,2,512]{2,1,0:T(2,128)(2,1)}), bf16[16,2,512]{2,1,0:T(2,128)(2,1)S(1)}, u32[]{:S(2)}, u32[]{:S(2)}) async-start(bf16[16,2,512]{2,1,0:T(2,128)(2,1)} %broadcast_select_fusion.3), calls=%async_computation.1 | async-start | bytes 65536 | tf_op jit(solution)/shard_map/all_to_all | solution.py:28
  47.8 2.3 %gather_fusion.5 = f32[512,512]{1,0:T(8,128)} fusion(f32[256,512]{1,0:T(8,128)S(1)} %fusion.38, s32[1024]{0:T(1024)S(1)} %pad_clamp_fusion), kind=kCustom, calls=%fused_computation.7.clone | custom fusion | bytes 2099200 | tf_op jit(solution)/shard_map/jit(_take)/gather | solution.py:33
  50.1 3.7 %all-to-all-done.1 = bf16[16,2,512]{2,1,0:T(2,128)(2,1)S(1)} async-done(((bf16[16,2,512]{2,1,0:T(2,128)(2,1)}), bf16[16,2,512]{2,1,0:T(2,128)(2,1)S(1)}, u32[]{:S(2)}, u32[]{:S(2)}) %all-to-all-start.1) | async-done | bytes 32800 | tf_op jit(solution)/shard_map/all_to_all | solution.py:28
  55.1 2.3 %gather_fusion.4 = f32[512,512]{1,0:T(8,128)} fusion(f32[288,512]{1,0:T(8,128)S(1)} %fusion.44, s32[1024]{0:T(1024)S(1)} %pad_clamp_fusion.1), kind=kCustom, calls=%fused_computation.5.clone | custom fusion | bytes 2099200 | tf_op jit(solution)/shard_map/jit(_take)/gather | solution.py:32
  57.4 3.4 %fusion.181 = (f32[512]{0:T(512)S(1)}, f32[512,512]{1,0:T(8,128)}) fusion(bf16[1,512,512]{2,1,0:T(8,128)(2,1)S(1)} %copy-done, f32[512,512]{1,0:T(8,128)} %gather_fusion.5, f32[512,512]{1,0:T(8,128)} %gather_fusion.4, f32[512]{0:T(512)S(1)} %bitcast.126, pred[512]{0:T(512)(128)(4,1)S(1)} %get-tuple-element.23, pred[512]{0:T(512)(128)(4,1)S(1)} %get-tuple-element.24, ...), kind=kOutput, calls=%fused_computation.212 | convolution fusion | flops 539753984 | bytes 4723712 | tf_op jit(solution)/shard_map/dot_general | solution.py:14
  60.8 1.5 %multiply_reduce_fusion.1 = f32[512]{0:T(512)S(1)} fusion(f32[512,512]{1,0:T(8,128)} %get-tuple-element.16, f32[512]{0:T(512)S(1)} %broadcast_multiply_fusion.1), kind=kLoop, calls=%fused_computation.36 | loop fusion | flops 785920 | bytes 1052672 | tf_op jit(solution)/shard_map/reduce_sum | solution.py:20
  62.3 2.8 %fusion.9 = f32[256,512]{1,0:T(8,128)} fusion(f32[512,512]{1,0:T(8,128)} %get-tuple-element.16, f32[512]{0:T(512)S(1)} %add_rsqrt_fusion.1, f32[512]{0:T(512)S(1)} %broadcast_multiply_fusion.1, f32[512]{0:T(512)S(1)} %fusion.155, f32[512]{0:T(512)S(1)} %bitcast.118, bf16[1,2,512,512]{3,2,1,0:T(8,128)(2,1)} %param.30, s32[512]{0:T(512)S(1)} %copy-done.24), kind=kOutput, calls=%fused_computation.28 | convolution fusion | flops 270008320 | bytes 2107392 | tf_op jit(solution)/shard_map/dot_general | solution.py:14
  65.2 2.4 %add_convert_fusion.1 = bf16[512,512]{1,0:T(8,128)(2,1)} fusion(f32[512,512]{1,0:T(8,128)} %get-tuple-element.16, f32[512]{0:T(512)S(1)} %add_rsqrt_fusion.1, f32[512]{0:T(512)S(1)} %broadcast_multiply_fusion.1, f32[512]{0:T(512)S(1)} %fusion.155, f32[512]{0:T(512)S(1)} %bitcast.119, bf16[768,512]{1,0:T(8,128)(2,1)S(1)} %broadcast_select_fusion.1), kind=kLoop, calls=%fused_computation.34 | loop fusion | flops 1835008 | bytes 2105344 | tf_op jit(solution)/shard_map/convert_element_type | solution.py:37
  67.6 2.6 %fusion.186 = (f32[256]{0:T(256)S(1)}, f32[256,512]{1,0:T(8,128)}) fusion(bf16[1,512,512]{2,1,0:T(8,128)(2,1)S(1)} %copy-done.21, f32[256,512]{1,0:T(8,128)} %fusion.9, bf16[1,2,512,512]{3,2,1,0:T(8,128)(2,1)} %param.30, f32[512]{0:T(512)S(1)} %bitcast.123, bf16[768,512]{1,0:T(8,128)(2,1)S(1)} %broadcast_select_fusion.1), kind=kOutput, calls=%fused_computation.213 | convolution fusion | flops 269483776 | bytes 2362368 | tf_op jit(solution)/shard_map/dot_general | solution.py:14
  70.1 1.3 %multiply_reduce_fusion.4 = f32[256]{0:T(256)S(1)} fusion(f32[256,512]{1,0:T(8,128)} %get-tuple-element.18, f32[256]{0:T(256)S(1)} %broadcast_multiply_fusion.4), kind=kLoop, calls=%fused_computation.100 | loop fusion | flops 392960 | bytes 526336 | tf_op jit(solution)/shard_map/reduce_sum | solution.py:20
  73.4 1.3 %collective-permute-start.1 = (bf16[768,512]{1,0:T(8,128)(2,1)S(1)}, bf16[768,512]{1,0:T(8,128)(2,1)}, u32[]{:S(2)}, u32[]{:S(2)}) collective-permute-start(bf16[768,512]{1,0:T(8,128)(2,1)S(1)} %pad_maximum_fusion.2), channel_id=1, source_target_pairs={{0,16},{1,17},{2,18},{3,19},{4,20},{5,21},{6,22},{7,23},{8,24},{9,... | collective-permute-start | bytes 2359304 | tf_op jit(solution)/shard_map/ppermute | solution.py:10
  74.7 3.4 %collective-permute-done.1 = bf16[768,512]{1,0:T(8,128)(2,1)} collective-permute-done((bf16[768,512]{1,0:T(8,128)(2,1)S(1)}, bf16[768,512]{1,0:T(8,128)(2,1)}, u32[]{:S(2)}, u32[]{:S(2)}) %collective-permute-start.1) | collective-permute-done | bytes 786464 | tf_op jit(solution)/shard_map/ppermute | solution.py:10
  78.1 1.4 %broadcast_select_fusion = bf16[768,512]{1,0:T(8,128)(2,1)S(1)} fusion(bf16[768,512]{1,0:T(8,128)(2,1)} %collective-permute-done.1, pred[]{:T(512)S(6)} %eq.19, bf16[512,512]{1,0:T(8,128)(2,1)S(1)} %copy-done.7, bf16[256,512]{1,0:T(8,128)(2,1)} %get-tuple-element.9), kind=kLoop, calls=%fused_computation.57 | loop fusion | flops 1966080 | bytes 2359297 | tf_op jit(solution)/shard_map/jit(_where)/select_n | solution.py:91
  80.9 3.7 %all-to-all-start.2 = ((bf16[16,2,512]{2,1,0:T(2,128)(2,1)}), bf16[16,2,512]{2,1,0:T(2,128)(2,1)S(1)}, u32[]{:S(2)}, u32[]{:S(2)}) async-start(bf16[16,2,512]{2,1,0:T(2,128)(2,1)} %broadcast_select_fusion.2), calls=%async_computation.2 | async-start | bytes 65536 | tf_op jit(solution)/shard_map/all_to_all | solution.py:28
  84.9 2.3 %gather_fusion.8 = f32[512,512]{1,0:T(8,128)} fusion(f32[256,512]{1,0:T(8,128)S(1)} %fusion.36, s32[1024]{0:T(1024)S(1)} %pad_clamp_fusion), kind=kCustom, calls=%fused_computation.8.clone | custom fusion | bytes 2099200 | tf_op jit(solution)/shard_map/jit(_take)/gather | solution.py:33
  87.2 3.4 %all-to-all-done.2 = bf16[16,2,512]{2,1,0:T(2,128)(2,1)S(1)} async-done(((bf16[16,2,512]{2,1,0:T(2,128)(2,1)}), bf16[16,2,512]{2,1,0:T(2,128)(2,1)S(1)}, u32[]{:S(2)}, u32[]{:S(2)}) %all-to-all-start.2) | async-done | bytes 32800 | tf_op jit(solution)/shard_map/all_to_all | solution.py:28
  91.9 2.3 %gather_fusion.7 = f32[512,512]{1,0:T(8,128)} fusion(f32[288,512]{1,0:T(8,128)S(1)} %fusion.42, s32[1024]{0:T(1024)S(1)} %pad_clamp_fusion.1), kind=kCustom, calls=%fused_computation.6.clone | custom fusion | bytes 2099200 | tf_op jit(solution)/shard_map/jit(_take)/gather | solution.py:32
  94.2 3.6 %fusion.191 = (f32[512]{0:T(512)S(1)}, f32[512,512]{0,1:T(8,128)}) fusion(bf16[1,512,512]{2,1,0:T(8,128)(2,1)S(1)} %copy-done, f32[512,512]{1,0:T(8,128)} %gather_fusion.8, f32[512,512]{1,0:T(8,128)} %gather_fusion.7, f32[512]{0:T(512)S(1)} %bitcast.127, pred[512]{0:T(512)(128)(4,1)S(1)} %get-tuple-element.23, pred[512]{0:T(512)(128)(4,1)S(1)} %get-tuple-element.24, ...), kind=kOutput, calls=%fused_computation.214 | convolution fusion | flops 539753984 | bytes 4723712 | tf_op jit(solution)/shard_map/dot_general | solution.py:14
  97.9 1.6 %copy.29 = f32[512,512]{1,0:T(8,128)S(1)} copy(f32[512,512]{0,1:T(8,128)} %get-tuple-element.20) | data formatting | bytes 2097152 | tf_op jit(solution)/shard_map/dot_general | solution.py:14
  99.7 2.5 %fusion.10 = f32[256,512]{1,0:T(8,128)} fusion(f32[512,512]{1,0:T(8,128)S(1)} %copy.29, f32[512]{0:T(512)S(1)} %add_rsqrt_fusion, f32[512]{0:T(512)S(1)} %broadcast_multiply_fusion, f32[512]{0:T(512)S(1)} %fusion.155, f32[512]{0:T(512)S(1)} %bitcast.120, bf16[1,2,512,512]{3,2,1,0:T(8,128)(2,1)} %param.30, s32[512]{0:T(512)S(1)} %copy-done.24), kind=kOutput, calls=%fused_computation.29 | convolution fusion | flops 270008320 | bytes 2107392 | tf_op jit(solution)/shard_map/dot_general | solution.py:14
  103.4 1.9 %fusion.196 = (f32[256]{0:T(256)S(1)}, f32[256,512]{1,0:T(8,128)S(1)}) fusion(bf16[1,512,512]{2,1,0:T(8,128)(2,1)S(1)} %copy-done.22, f32[256,512]{1,0:T(8,128)} %fusion.10, bf16[1,2,512,512]{3,2,1,0:T(8,128)(2,1)} %param.30, f32[512]{0:T(512)S(1)} %bitcast.124, bf16[768,512]{1,0:T(8,128)(2,1)S(1)} %copy-done.3), kind=kOutput, calls=%fused_computation.215 | convolution fusion | flops 269483776 | bytes 2362368 | tf_op jit(solution)/shard_map/dot_general | solution.py:14
  (125 shorter events, 21.5 us)
Async XLA Ops:
  0.6 24.6 %copy-start = (bf16[1,512,512]{2,1,0:T(8,128)(2,1)S(1)}, bf16[1,512,512]{2,1,0:T(8,128)(2,1)}, u32[]{:S(2)}) copy-start(bf16[1,512,512]{2,1,0:T(8,128)(2,1)} %param.28) | copy-start | bytes 1572868
  0.6 3.5 %copy-start.20 = (bf16[2,256,512]{2,1,0:T(8,128)(2,1)S(1)}, bf16[2,256,512]{2,1,0:T(8,128)(2,1)}, u32[]{:S(2)}) copy-start(bf16[2,256,512]{2,1,0:T(8,128)(2,1)} %param.20) | copy-start | bytes 1572868
  5.0 10.4 %copy-start.23 = (s32[512]{0:T(512)S(1)}, s32[512]{0:T(512)}, u32[]{:S(2)}) copy-start(s32[512]{0:T(512)} %param.22) | copy-start | bytes 6148
  5.0 10.4 %copy-start.24 = (s32[512]{0:T(512)S(1)}, s32[512]{0:T(512)}, u32[]{:S(2)}) copy-start(s32[512]{0:T(512)} %param.23) | copy-start | bytes 6148
  5.0 10.5 %copy-start.1 = (bf16[1,3,512,512]{3,2,1,0:T(8,128)(2,1)S(1)}, bf16[1,3,512,512]{3,2,1,0:T(8,128)(2,1)}, u32[]{:S(2)}) copy-start(bf16[1,3,512,512]{3,2,1,0:T(8,128)(2,1)} %param.26) | copy-start | bytes 4718596
  6.2 9.6 %copy-start.25 = (bf16[1,512]{1,0:T(2,128)(2,1)S(1)}, bf16[1,512]{1,0:T(2,128)(2,1)}, u32[]{:S(2)}) copy-start(bf16[1,512]{1,0:T(2,128)(2,1)} %param.27) | copy-start | bytes 3076
  6.2 9.2 %copy-start.16 = (bf16[256,512]{1,0:T(8,128)(2,1)}, bf16[256,512]{1,0:T(8,128)(2,1)S(1)}, u32[]{:S(2)}) copy-start(bf16[256,512]{1,0:T(8,128)(2,1)S(1)} %slice.103) | copy-start | bytes 786436
  6.4 12.1 %copy-start.26 = (bf16[1,512]{1,0:T(2,128)(2,1)S(1)}, bf16[1,512]{1,0:T(2,128)(2,1)}, u32[]{:S(2)}) copy-start(bf16[1,512]{1,0:T(2,128)(2,1)} %param.29) | copy-start | bytes 3076
  6.5 12.2 %copy-start.27 = (bf16[1,512]{1,0:T(2,128)(2,1)S(1)}, bf16[1,512]{1,0:T(2,128)(2,1)}, u32[]{:S(2)}) copy-start(bf16[1,512]{1,0:T(2,128)(2,1)} %param.31) | copy-start | bytes 3076
  6.5 12.2 %copy-start.28 = (bf16[1,512]{1,0:T(2,128)(2,1)S(1)}, bf16[1,512]{1,0:T(2,128)(2,1)}, u32[]{:S(2)}) copy-start(bf16[1,512]{1,0:T(2,128)(2,1)} %param.33) | copy-start | bytes 3076
  7.9 13.7 %all-to-all-start = ((bf16[16,2,512]{2,1,0:T(2,128)(2,1)}), bf16[16,2,512]{2,1,0:T(2,128)(2,1)S(1)}, u32[]{:S(2)}, u32[]{:S(2)}) async-start(bf16[16,2,512]{2,1,0:T(2,128)(2,1)} %broadcast_select_fusion.4), calls=%async_computation | async-start | bytes 65536 | tf_op jit(solution)/shard_map/all_to_all | solution.py:28
  28.7 1.6 %copy-start.10 = (f32[512,512]{1,0:T(8,128)S(1)}, f32[512,512]{1,0:T(8,128)}, u32[]{:S(2)}) copy-start(f32[512,512]{1,0:T(8,128)} %get-tuple-element.12) | copy-start | bytes 3145732
  30.6 5.1 %copy-start.4 = (bf16[512,512]{1,0:T(8,128)(2,1)}, bf16[512,512]{1,0:T(8,128)(2,1)S(1)}, u32[]{:S(2)}) copy-start(bf16[512,512]{1,0:T(8,128)(2,1)S(1)} %add_convert_fusion.2) | copy-start | bytes 1572868
  35.3 5.7 %copy-start.6 = (bf16[512,512]{1,0:T(8,128)(2,1)S(1)}, bf16[512,512]{1,0:T(8,128)(2,1)}, u32[]{:S(2)}) copy-start(bf16[512,512]{1,0:T(8,128)(2,1)} %get-tuple-element.7) | copy-start | bytes 1572868
  35.3 5.7 %copy-start.11 = (bf16[256,512]{1,0:T(8,128)(2,1)S(1)}, bf16[256,512]{1,0:T(8,128)(2,1)}, u32[]{:S(2)}) copy-start(bf16[256,512]{1,0:T(8,128)(2,1)} %get-tuple-element.9) | copy-start | bytes 786436
  35.7 5.2 %copy-start.12 = (bf16[256,512]{1,0:T(8,128)(2,1)}, bf16[256,512]{1,0:T(8,128)(2,1)S(1)}, u32[]{:S(2)}) copy-start(bf16[256,512]{1,0:T(8,128)(2,1)S(1)} %add_convert_fusion.5) | copy-start | bytes 786436
  35.8 5.2 %collective-permute-start = (bf16[768,512]{1,0:T(8,128)(2,1)S(1)}, bf16[768,512]{1,0:T(8,128)(2,1)S(1)}, u32[]{:S(2)}, u32[]{:S(2)}) collective-permute-start(bf16[768,512]{1,0:T(8,128)(2,1)S(1)} %pad_maximum_fusion.1), channel_id=1, source_target_pairs={{0,16},{1,17},{2,18},{3,19},{4,20},{5,21},{6,22},{7,23},{8,24},{9,... | collective-permute-start | bytes 2359304 | tf_op jit(solution)/shard_map/ppermute | solution.py:10
  41.2 1.4 %copy-start.18 = (bf16[256,512]{1,0:T(8,128)(2,1)}, bf16[256,512]{1,0:T(8,128)(2,1)S(1)}, u32[]{:S(2)}) copy-start(bf16[256,512]{1,0:T(8,128)(2,1)S(1)} %slice.105) | copy-start | bytes 786436
  42.6 11.2 %all-to-all-start.1 = ((bf16[16,2,512]{2,1,0:T(2,128)(2,1)}), bf16[16,2,512]{2,1,0:T(2,128)(2,1)S(1)}, u32[]{:S(2)}, u32[]{:S(2)}) async-start(bf16[16,2,512]{2,1,0:T(2,128)(2,1)} %broadcast_select_fusion.3), calls=%async_computation.1 | async-start | bytes 65536 | tf_op jit(solution)/shard_map/all_to_all | solution.py:28
  65.2 2.4 %copy-start.21 = (bf16[1,512,512]{2,1,0:T(8,128)(2,1)S(1)}, bf16[1,512,512]{2,1,0:T(8,128)(2,1)}, u32[]{:S(2)}) copy-start(bf16[1,512,512]{2,1,0:T(8,128)(2,1)} %param.32) | copy-start | bytes 1572868
  70.1 2.6 %copy-start.8 = (bf16[512,512]{1,0:T(8,128)(2,1)S(1)}, bf16[512,512]{1,0:T(8,128)(2,1)}, u32[]{:S(2)}) copy-start(bf16[512,512]{1,0:T(8,128)(2,1)} %add_convert_fusion.1) | copy-start | bytes 1572868
  70.1 8.0 %copy-start.7 = (bf16[512,512]{1,0:T(8,128)(2,1)S(1)}, bf16[512,512]{1,0:T(8,128)(2,1)}, u32[]{:S(2)}) copy-start(bf16[512,512]{1,0:T(8,128)(2,1)} %get-tuple-element.7) | copy-start | bytes 1572868
  73.4 4.7 %collective-permute-start.1 = (bf16[768,512]{1,0:T(8,128)(2,1)S(1)}, bf16[768,512]{1,0:T(8,128)(2,1)}, u32[]{:S(2)}, u32[]{:S(2)}) collective-permute-start(bf16[768,512]{1,0:T(8,128)(2,1)S(1)} %pad_maximum_fusion.2), channel_id=1, source_target_pairs={{0,16},{1,17},{2,18},{3,19},{4,20},{5,21},{6,22},{7,23},{8,24},{9,... | collective-permute-start | bytes 2359304 | tf_op jit(solution)/shard_map/ppermute | solution.py:10
  79.5 14.7 %copy-start.2 = (bf16[768,512]{1,0:T(8,128)(2,1)}, bf16[768,512]{1,0:T(8,128)(2,1)S(1)}, u32[]{:S(2)}) copy-start(bf16[768,512]{1,0:T(8,128)(2,1)S(1)} %broadcast_select_fusion) | copy-start | bytes 2359300
  79.6 1.4 %copy-start.17 = (bf16[256,512]{1,0:T(8,128)(2,1)}, bf16[256,512]{1,0:T(8,128)(2,1)S(1)}, u32[]{:S(2)}) copy-start(bf16[256,512]{1,0:T(8,128)(2,1)S(1)} %slice.107) | copy-start | bytes 786436
  80.9 9.7 %all-to-all-start.2 = ((bf16[16,2,512]{2,1,0:T(2,128)(2,1)}), bf16[16,2,512]{2,1,0:T(2,128)(2,1)S(1)}, u32[]{:S(2)}, u32[]{:S(2)}) async-start(bf16[16,2,512]{2,1,0:T(2,128)(2,1)} %broadcast_select_fusion.2), calls=%async_computation.2 | async-start | bytes 65536 | tf_op jit(solution)/shard_map/all_to_all | solution.py:28
  99.4 2.8 %copy-start.3 = (bf16[768,512]{1,0:T(8,128)(2,1)S(1)}, bf16[768,512]{1,0:T(8,128)(2,1)}, u32[]{:S(2)}) copy-start(bf16[768,512]{1,0:T(8,128)(2,1)} %copy-done.2) | copy-start | bytes 2359300
  102.2 1.1 %copy-start.22 = (bf16[1,512,512]{2,1,0:T(8,128)(2,1)S(1)}, bf16[1,512,512]{2,1,0:T(8,128)(2,1)}, u32[]{:S(2)}) copy-start(bf16[1,512,512]{2,1,0:T(8,128)(2,1)} %param.32) | copy-start | bytes 1572868
  103.4 2.4 %copy-start.19 = (bf16[1,512,512]{2,1,0:T(8,128)(2,1)S(1)}, bf16[1,512,512]{2,1,0:T(8,128)(2,1)}, u32[]{:S(2)}) copy-start(bf16[1,512,512]{2,1,0:T(8,128)(2,1)} %fusion.23) | copy-start | bytes 1572868
  105.3 1.2 %copy-start.9 = (bf16[512,512]{1,0:T(8,128)(2,1)S(1)}, bf16[512,512]{1,0:T(8,128)(2,1)}, u32[]{:S(2)}) copy-start(bf16[512,512]{1,0:T(8,128)(2,1)} %add_convert_fusion.1) | copy-start | bytes 1572868
  105.3 1.3 %copy-start.13 = (bf16[256,512]{1,0:T(8,128)(2,1)S(1)}, bf16[256,512]{1,0:T(8,128)(2,1)}, u32[]{:S(2)}) copy-start(bf16[256,512]{1,0:T(8,128)(2,1)} %copy-done.12) | copy-start | bytes 786436
  105.3 1.3 %copy-start.15 = (bf16[256,512]{1,0:T(8,128)(2,1)S(1)}, bf16[256,512]{1,0:T(8,128)(2,1)}, u32[]{:S(2)}) copy-start(bf16[256,512]{1,0:T(8,128)(2,1)} %copy-done.14) | copy-start | bytes 786436
  (2 other events, 1.8 us)
where the time goes:
time: 111 us; the launch traced here: 109 us
  matrix products  31.8 us (29%)
  local copies, waits for them, and re-layouts  24.2 us (22%)
  starting transfers between devices  18.5 us (17%)
  other arithmetic  17.7 us (16%)
  waiting for transfers between devices  15 us (14%)
  between operations  1.95 us (2%)
    dot_general x16, matrix products, project(): return jnp.dot(values, weight, preferred_element_type=jnp.float32)  31.8 us
    all_to_all x3, starting transfers between devices, apply_layer(): lax.all_to_all(outgoing, 'dom', split_axis=0, concat_axis=0, tiled=True)  15.9 us
    all_to_all x3, waiting for transfers between devices, apply_layer(): lax.all_to_all(outgoing, 'dom', split_axis=0, concat_axis=0, tiled=True)  7.73 us
    ppermute x2, waiting for transfers between devices, from_behind(): return lax.ppermute(block, axis, route)  7.25 us
    gather x3, local copies, waits for them, and re-layouts, apply_layer(): jnp.take(from_receiver, edge_dst, axis=0)  6.98 us
    gather x3, local copies, waits for them, and re-layouts, apply_layer(): jnp.take(from_sender, edge_src, axis=0)  6.97 us
    reduce_sum x6, other arithmetic, layer_norm(): row_var = jnp.mean(centred * centred, axis=-1, keepdims=True)  5.01 us
    squeeze x2, local copies, waits for them, and re-layouts, local(): fresh_input = jnp.concatenate([node_feats[pick], edge_feats[pick]], axis=0)  2.88 us
  transfers between devices with their start and end apart: 5, of which 5 were waited for; matrix products, arithmetic and copies ran while one was open for 9% of the time, Pallas kernels for 0%

commit v1 on v0

v1 whole, which is shorter than its diff:
```python
import functools

import jax
import jax.numpy as jnp
from jax import lax
from jax.experimental import pallas as pl
from jax.experimental.pallas import tpu as pltpu
from jax.sharding import PartitionSpec as P

F32 = jnp.float32
BF16 = jnp.bfloat16
LANES = 128
BLOCK = 256


def dot(lhs, rhs):
    return jnp.dot(lhs, rhs, preferred_element_type=F32)


def silu(x):
    half = 0.5 * x
    return half + half * jnp.tanh(half)


def layer_norm(values, gain):
    row_mean = jnp.mean(values, axis=-1, keepdims=True)
    centred = values - row_mean
    row_var = jnp.mean(centred * centred, axis=-1, keepdims=True)
    return centred * lax.rsqrt(row_var + 1e-05) * gain


def column(row):
    return jnp.broadcast_to(row, (LANES, row.shape[1])).T


def onehot(col, width):
    parts = []
    for start in range(0, width, LANES):
        size = min(LANES, width - start)
        lane = lax.broadcasted_iota(jnp.int32, (col.shape[0], size), 1) + start
        parts.append((col[:, :size] == lane).astype(F32).astype(BF16))
    return parts[0] if len(parts) == 1 else jnp.concatenate(parts, axis=1)


def kernel(peers, hcap, chunks,
           cnt, src, dst, send, eb1, eg, nb1, ng,
           nf, ef, ew1, ew2, nw1, nw2,
           no, eo,
           nl, el, onl, oel, rhs, w1r, w2, n1, n2, msg, ohs, ohr, ohrt,
           out0, out1, halo, hx,
           wsem, lsem, hsem, osem, s0sem, s1sem, ssem):
    batches, nodes, width = nl.shape
    edges = el.shape[1]
    halo_rows = peers * hcap
    sec = lax.axis_index("section")
    me = lax.axis_index("dom")
    barrier = pltpu.get_barrier_semaphore()

    def hail(section, target):
        pl.semaphore_signal(barrier, inc=1, device_id={"section": section, "dom": target},
                            device_id_type=pl.DeviceIdType.MESH)

    def peer(step):
        return lax.rem(me + step, peers)

    @pl.loop(0, peers)
    def _(step):
        hail(1 - sec, peer(step))

    @pl.when(sec == 0)
    def _():
        @pl.loop(1, peers)
        def _(step):
            hail(0, peer(step))

    at_e, at_r, at_s = nodes, nodes + width, 2 * nodes + width

    def load(index, source, target):
        return pltpu.make_async_copy(source, target, wsem.at[index])

    weights = [
        load(0, ew1.at[0, 1], rhs.at[pl.ds(at_s, width)]),
        load(1, ew1.at[0, 2], w1r),
        load(2, ew1.at[0, 0], rhs.at[pl.ds(at_e, width)]),
        load(3, ew2.at[0], w2),
        load(4, nw1.at[0, 0], n1.at[pl.ds(0, width)]),
        load(5, nw1.at[0, 1], n1.at[pl.ds(width, width)]),
        load(6, nw2.at[0], n2),
    ]

    def node_in(m):
        return pltpu.make_async_copy(nf.at[m], nl.at[m], lsem.at[m, 0])

    def edge_in(m, c):
        lo, hi = chunks[c]
        return pltpu.make_async_copy(ef.at[m, pl.ds(lo, hi - lo)], el.at[m, pl.ds(lo, hi - lo)],
                                     lsem.at[m, 1 + c])

    @pl.when(sec == 0)
    def _():
        for m in range(batches):
            node_in(m).start()

    for copy in weights[:3]:
        copy.start()

    @pl.when(sec == 0)
    def _():
        for c in range(len(chunks)):
            edge_in(0, c).start()

    for copy in weights[3:]:
        copy.start()

    @pl.when(sec == 0)
    def _():
        for m in range(1, batches):
            for c in range(len(chunks)):
                edge_in(m, c).start()

    send_hot = jnp.concatenate(
        [(lax.broadcasted_iota(jnp.int32, (peers, nodes), 1) == send[:, k:k + 1]).astype(F32)
         for k in range(hcap)], axis=0).astype(BF16)

    def gather_rows(values, store):
        rows = dot(send_hot, values)
        for t in range(peers):
            for k in range(hcap):
                store(t, k, rows[k * peers + t:k * peers + t + 1])

    @pl.when(sec == 0)
    def _():
        for m in range(batches):
            node_in(m).wait()

            def store(t, k, row, m=m):
                out0[t, m, pl.ds(k, 1)] = row

            gather_rows(nl[m], store)
        pl.semaphore_wait(barrier, 2 * peers - 1)

        @pl.loop(1, peers)
        def _(step):
            target = peer(step)
            pltpu.make_async_remote_copy(
                src_ref=out0.at[target], dst_ref=halo.at[me], send_sem=s0sem, recv_sem=hsem.at[0],
                device_id={"section": 0, "dom": target}, device_id_type=pl.DeviceIdType.MESH).start()

        pltpu.make_async_copy(out0.at[me], halo.at[me], hsem.at[0]).start()

    @pl.when(sec == 1)
    def _():
        pl.semaphore_wait(barrier, peers)

    col_s = column(src[...])
    col_r = column(dst[...])
    ohs[...] = onehot(col_s, nodes)
    ohr[...] = onehot(col_r, nodes)
    ohrt[...] = (lax.broadcasted_iota(jnp.int32, (nodes, edges), 0) == dst[...]).astype(F32).astype(BF16)
    halo_hot = onehot(col_s[:halo_rows] - nodes, halo_rows)

    bias_e = eb1[...].astype(F32)
    gain_e = eg[...].astype(F32)
    bias_n = nb1[...].astype(F32)
    gain_n = ng[...].astype(F32)
    live = cnt[0]

    def to_next(m, slot, source, target):
        return pltpu.make_async_remote_copy(
            src_ref=source, dst_ref=target, send_sem=ssem.at[m, slot], recv_sem=lsem.at[m, slot],
            device_id={"section": 1, "dom": me}, device_id_type=pl.DeviceIdType.MESH)

    def node_next(m):
        return to_next(m, 0, onl.at[m], nl.at[m])

    def edge_next(m, c):
        lo, hi = chunks[c]
        rows = pl.ds(lo, hi - lo)
        return to_next(m, 1 + c, oel.at[m, rows], el.at[m, rows])

    def node_res(m):
        return pltpu.make_async_copy(onl.at[m], no.at[0, m], osem.at[m, 0])

    def edge_res(m, c):
        lo, hi = chunks[c]
        rows = pl.ds(lo, hi - lo)
        return pltpu.make_async_copy(oel.at[m, rows], eo.at[0, m, rows], osem.at[m, 1 + c])

    for m in range(batches):
        @pl.when(sec == 1)
        def _():
            node_in(m).wait()

        if m == 0:
            weights[0].wait()
            weights[1].wait()
        values = nl[m]
        rhs[:nodes] = dot(values, rhs[at_s:]).astype(BF16)
        rhs[at_r:at_s] = dot(values, w1r[...]).astype(BF16)

        for c in list(range(1, len(chunks))) + [0]:
            lo, hi = chunks[c]
            edge_in(m, c).wait()
            if m == 0 and c == 1:
                weights[2].wait()
                weights[3].wait()
            if c == 0:
                if m == 0:
                    @pl.when(sec == 0)
                    def _():
                        pltpu.make_async_copy(halo, halo, hsem.at[0]).wait()

                @pl.when(sec == 1)
                def _():
                    pltpu.make_async_copy(halo.at[:, m], halo.at[:, m], hsem.at[m]).wait()

                for p in range(peers):
                    hx[pl.ds(p * hcap, hcap)] = halo[p, m]
                from_far = dot(halo_hot, hx[...].astype(BF16)).astype(BF16)
                lat = el[m, lo:hi]
                lhs = jnp.concatenate([lat, ohr[lo:hi], from_far], axis=1)
                pre = dot(lhs, rhs[at_e:])
            else:
                lat = el[m, lo:hi]
                lhs = jnp.concatenate([ohs[lo:hi], lat, ohr[lo:hi]], axis=1)
                pre = dot(lhs, rhs[:at_s])
            hidden = silu(pre + bias_e).astype(BF16)
            update = layer_norm(dot(hidden, w2[...]), gain_e)
            slot = lax.broadcasted_iota(jnp.int32, (hi - lo, 1), 0) + lo
            update = update * (slot < live).astype(F32)
            msg[lo:hi] = update.astype(BF16)
            oel[m, lo:hi] = (lat.astype(F32) + update).astype(BF16)

            @pl.when(sec == 0)
            def _():
                edge_next(m, c).start()

            edge_res(m, c).start()

        if m == 0:
            for copy in weights[4:]:
                copy.wait()
        incoming = dot(ohrt[...], msg[...]).astype(BF16)
        values = nl[m]
        pre = dot(jnp.concatenate([values, incoming], axis=1), n1[...])
        hidden = silu(pre + bias_n).astype(BF16)
        update = layer_norm(dot(hidden, n2[...]), gain_n)
        onl[m] = (values.astype(F32) + update).astype(BF16)

        @pl.when(sec == 0)
        def _():
            node_next(m).start()

            def store(t, k, row):
                out1[m, t, pl.ds(k, 1)] = row

            gather_rows(onl[m], store)

            @pl.loop(0, peers)
            def _(step):
                target = peer(step)
                pltpu.make_async_remote_copy(
                    src_ref=out1.at[m, target], dst_ref=halo.at[me, m], send_sem=s1sem.at[m],
                    recv_sem=hsem.at[m], device_id={"section": 1, "dom": target},
                    device_id_type=pl.DeviceIdType.MESH).start()

        node_res(m).start()

    for m in range(batches):
        node_res(m).wait()
        for c in range(len(chunks)):
            edge_res(m, c).wait()

    @pl.when(sec == 0)
    def _():
        others = out0.at[pl.ds(0, peers - 1)]
        pltpu.make_async_copy(others, others, s0sem).wait()
        for m in range(batches):
            pltpu.make_async_copy(out1.at[m], out1.at[m], s1sem.at[m]).wait()
            node_next(m).wait_send()
            for c in range(len(chunks)):
                edge_next(m, c).wait_send()


def local(node_feats, edge_feats, edge_src, edge_dst, edge_count, send_rows,
          edge_w1, edge_b1, edge_w2, edge_gain, node_w1, node_b1, node_w2, node_gain):
    batches, nodes, width = node_feats.shape
    edges = edge_feats.shape[1]
    peers, hcap = send_rows.shape
    inner = edge_w2.shape[1]
    halo_rows = peers * hcap
    chunks = [(0, halo_rows)]
    while chunks[-1][1] < edges:
        start = chunks[-1][1]
        chunks.append((start, min(edges, (start // BLOCK + 1) * BLOCK)))
    slots = len(chunks) + 1
    anywhere = pl.BlockSpec(memory_space=pl.ANY)
    vmem = pl.BlockSpec(memory_space=pltpu.VMEM)
    dma = pltpu.SemaphoreType.DMA
    flops = 2 * batches * width * inner * (3 * edges + 6 * nodes)
    moved = 2 * (2 * batches * (nodes + edges) * width + 7 * width * inner)
    return pl.pallas_call(
        functools.partial(kernel, peers, hcap, chunks),
        out_shape=(jax.ShapeDtypeStruct((1, batches, nodes, width), BF16),
                   jax.ShapeDtypeStruct((1, batches, edges, width), BF16)),
        in_specs=[pl.BlockSpec(memory_space=pltpu.SMEM)] + [vmem] * 7 + [anywhere] * 6,
        out_specs=(anywhere, anywhere),
        scratch_shapes=[
            pltpu.VMEM((batches, nodes, width), BF16),
            pltpu.VMEM((batches, edges, width), BF16),
            pltpu.VMEM((batches, nodes, width), BF16),
            pltpu.VMEM((batches, edges, width), BF16),
            pltpu.VMEM((2 * nodes + 2 * width, inner), BF16),
            pltpu.VMEM((width, inner), BF16),
            pltpu.VMEM((inner, width), BF16),
            pltpu.VMEM((2 * width, inner), BF16),
            pltpu.VMEM((inner, width), BF16),
            pltpu.VMEM((edges, width), BF16),
            pltpu.VMEM((edges, nodes), BF16),
            pltpu.VMEM((edges, nodes), BF16),
            pltpu.VMEM((nodes, edges), BF16),
            pltpu.VMEM((peers, batches, hcap, width), F32),
            pltpu.VMEM((batches, peers, hcap, width), F32),
            pltpu.VMEM((peers, batches, hcap, width), F32),
            pltpu.VMEM((halo_rows, width), F32),
            dma((7,)),
            dma((batches, slots)),
            dma((batches,)),
            dma((batches, slots)),
            dma,
            dma((batches,)),
            dma((batches, slots)),
        ],
        compiler_params=pltpu.CompilerParams(
            collective_id=0, has_side_effects=True, vmem_limit_bytes=48 * 1024 * 1024),
        cost_estimate=pl.CostEstimate(flops=flops, bytes_accessed=moved, transcendentals=0),
    )(edge_count, edge_src.reshape(1, -1), edge_dst.reshape(1, -1), send_rows,
      edge_b1, edge_gain, node_b1, node_gain,
      node_feats, edge_feats, edge_w1, edge_w2, node_w1, node_w2)


def solution(mesh):
    in_specs = (
        P(None, "dom", None),
        P(None, "dom", None),
        P("dom"),
        P("dom"),
        P("dom"),
        P("dom", None),
        P("section", None, None, None),
        P("section", None),
        P("section", None, None),
        P("section", None),
        P("section", None, None, None),
        P("section", None),
        P("section", None, None),
        P("section", None),
    )
    out_specs = (P("section", None, "dom", None), P("section", None, "dom", None))
    return jax.shard_map(local, mesh=mesh, in_specs=in_specs, out_specs=out_specs, check_vma=False)
```

time: 111 us -> 38.9 us (0.35); the launches traced: 109 us -> 38.4 us
  matrix products: 31.8 us -> 0 us
  Pallas kernels: 0 us -> 24.9 us
  starting transfers between devices: 18.5 us -> 0 us
  other arithmetic: 17.7 us -> 0 us
  waiting for transfers between devices: 15 us -> 0 us
  local copies, waits for them, and re-layouts: 24.2 us -> 12.2 us
    dot_general x16 -> x0, matrix products: 31.8 us -> none  [project(): return jnp.dot(values, weight, preferred_element_type=jnp.float32)]
    pallas_call x0 -> x1, Pallas kernels: none -> 24.9 us  [local(): pl.pallas_call(functools.partial(kernel, peers, hcap, chunks), out_shape=...]
    all_to_all x3 -> x0, starting transfers between devices: 15.9 us -> none  [apply_layer(): lax.all_to_all(outgoing, 'dom', split_axis=0, concat_axis=0, tiled=True)]
    gather x12 -> x0, local copies, waits for them, and re-layouts: 15.9 us -> none  [the longest x3 6.98 us: apply_layer(): jnp.take(from_receiver, edge_dst, axis=0)]
    unnamed x58 -> x25, local copies, waits for them, and re-layouts: 1.65 us -> 12.2 us
    all_to_all x3 -> x0, waiting for transfers between devices: 7.73 us -> none  [apply_layer(): lax.all_to_all(outgoing, 'dom', split_axis=0, concat_axis=0, tiled=True)]
    ppermute x2 -> x0, waiting for transfers between devices: 7.25 us -> none  [from_behind(): return lax.ppermute(block, axis, route)]
    select_n x10 -> x0, other arithmetic: 6.23 us -> none  [the longest x4 2.88 us: apply_layer(): outgoing = jnp.take(node_lat, send_rows, axis=0)]
  transfers between devices with their start and end apart: 5 -> 0, of which waited for: 5 -> 0; matrix products, arithmetic and copies ran while one was open for 9% -> 0% of each run, Pallas kernels for 0% -> 0%
where the time goes in v1:
time: 38.9 us; the launch traced here: 38.4 us
  Pallas kernels  24.9 us (64%)
  local copies, waits for them, and re-layouts  12.2 us (31%)
  between operations  1.3 us (3%)
    pallas_call x1, Pallas kernels, local(): pl.pallas_call(functools.partial(kernel, peers, hcap, chunks), out_shape=...  24.9 us
    unnamed x25, local copies, waits for them, and re-layouts  12.2 us

profile of v1, /device:TPU:1, one launch (start us, length us, event | category | flops | bytes accessed | tf_op | source)
XLA Modules:
  0.0 38.4 jit_solution(14640290722025160476)
XLA Ops:
  1.3 0.8 %copy.16.send = s32[16,2]{1,0:T(8,128)S(1)} copy(s32[16,2]{0,1:T(2,128)} %param.19) | data formatting | bytes 256 | tf_op args[5]
  2.0 0.0 copy-start
  2.0 1.2 %copy-done = bf16[2,512,512]{2,1,0:T(8,128)(2,1)S(1)} copy-done((bf16[2,512,512]{2,1,0:T(8,128)(2,1)S(1)}, bf16[2,512,512]{2,1,0:T(8,128)(2,1)}, u32[]{:S(2)}) %copy-start) | copy-done | bytes 1048600
  3.3 0.0 copy-start.1
  3.3 1.2 %copy-done.1 = bf16[1,2,512,512]{3,2,1,0:T(8,128)(2,1)S(1)} copy-done((bf16[1,2,512,512]{3,2,1,0:T(8,128)(2,1)S(1)}, bf16[1,2,512,512]{3,2,1,0:T(8,128)(2,1)}, u32[]{:S(2)}) %copy-start.1) | copy-done | bytes 1048600
  4.5 0.0 copy-start.2
  4.5 1.0 %copy-done.2 = bf16[2,256,512]{2,1,0:T(8,128)(2,1)S(1)} copy-done((bf16[2,256,512]{2,1,0:T(8,128)(2,1)S(1)}, bf16[2,256,512]{2,1,0:T(8,128)(2,1)}, u32[]{:S(2)}) %copy-start.2) | copy-done | bytes 524312
  5.5 0.0 copy-start.3
  5.5 1.0 %copy-done.3 = bf16[1,512,512]{2,1,0:T(8,128)(2,1)S(1)} copy-done((bf16[1,512,512]{2,1,0:T(8,128)(2,1)S(1)}, bf16[1,512,512]{2,1,0:T(8,128)(2,1)}, u32[]{:S(2)}) %copy-start.3) | copy-done | bytes 524312
  6.6 0.0 copy-start.4
  6.6 1.0 %copy-done.4 = bf16[1,512,512]{2,1,0:T(8,128)(2,1)S(1)} copy-done((bf16[1,512,512]{2,1,0:T(8,128)(2,1)S(1)}, bf16[1,512,512]{2,1,0:T(8,128)(2,1)}, u32[]{:S(2)}) %copy-start.4) | copy-done | bytes 524312
  7.6 0.0 copy-start.5
  7.6 0.7 %copy-done.5 = s32[512]{0:T(512)S(1)} copy-done((s32[512]{0:T(512)S(1)}, s32[512]{0:T(512)}, u32[]{:S(2)}) %copy-start.5) | copy-done | bytes 2072
  8.3 0.0 copy-start.6
  8.3 0.7 %copy-done.6 = s32[512]{0:T(512)S(1)} copy-done((s32[512]{0:T(512)S(1)}, s32[512]{0:T(512)}, u32[]{:S(2)}) %copy-start.6) | copy-done | bytes 2072
  9.0 0.0 copy-start.7
  9.0 0.7 %copy-done.7 = bf16[1,512]{1,0:T(2,128)(2,1)S(1)} copy-done((bf16[1,512]{1,0:T(2,128)(2,1)S(1)}, bf16[1,512]{1,0:T(2,128)(2,1)}, u32[]{:S(2)}) %copy-start.7) | copy-done | bytes 1048
  9.7 0.0 copy-start.8
  9.7 0.7 %copy-done.8 = bf16[1,512]{1,0:T(2,128)(2,1)S(1)} copy-done((bf16[1,512]{1,0:T(2,128)(2,1)S(1)}, bf16[1,512]{1,0:T(2,128)(2,1)}, u32[]{:S(2)}) %copy-start.8) | copy-done | bytes 1048
  10.3 0.0 copy-start.9
  10.3 0.7 %copy-done.9 = bf16[1,512]{1,0:T(2,128)(2,1)S(1)} copy-done((bf16[1,512]{1,0:T(2,128)(2,1)S(1)}, bf16[1,512]{1,0:T(2,128)(2,1)}, u32[]{:S(2)}) %copy-start.9) | copy-done | bytes 1048
  11.0 0.0 copy-start.10
  11.0 0.7 %copy-done.10 = bf16[1,512]{1,0:T(2,128)(2,1)S(1)} copy-done((bf16[1,512]{1,0:T(2,128)(2,1)S(1)}, bf16[1,512]{1,0:T(2,128)(2,1)}, u32[]{:S(2)}) %copy-start.10) | copy-done | bytes 1048
  11.7 24.9 %shard_map.149 = (bf16[1,2,256,512]{3,2,1,0:T(8,128)(2,1)S(1)}, bf16[1,2,512,512]{3,2,1,0:T(8,128)(2,1)S(1)}) custom-call(s32[1]{0:T(128)S(6)} %copy.19.cnt, s32[1,512]{1,0:T(1,128)S(1)} %bitcast.2, s32[1,512]{1,0:T(1,128)S(1)} %bitcast.3, s32[16,2]{1,0:T(8,128)S(1)} %copy.16.send, bf16[1,512]{1,0:T(2,128)(2,1)S(1)} %copy-done.7, ...), custom_call_target="tpu_custom_call" | custom-call | flops 3221225472 | bytes 6815744 | tf_op jit(solution)/shard_map/pallas_call | solution.py:302
  36.7 0.8 %copy.20 = bf16[1,2,256,512]{3,2,1,0:T(8,128)(2,1)} copy(bf16[1,2,256,512]{3,2,1,0:T(8,128)(2,1)S(1)} %get-tuple-element.4) | data formatting | bytes 1048576
  37.5 1.0 %copy.21 = bf16[1,2,512,512]{3,2,1,0:T(8,128)(2,1)} copy(bf16[1,2,512,512]{3,2,1,0:T(8,128)(2,1)S(1)} %get-tuple-element.5) | data formatting | bytes 2097152
Async XLA Ops:
  2.0 1.2 %copy-start = (bf16[2,512,512]{2,1,0:T(8,128)(2,1)S(1)}, bf16[2,512,512]{2,1,0:T(8,128)(2,1)}, u32[]{:S(2)}) copy-start(bf16[2,512,512]{2,1,0:T(8,128)(2,1)} %ef.1) | copy-start | bytes 3145732
  3.3 1.2 %copy-start.1 = (bf16[1,2,512,512]{3,2,1,0:T(8,128)(2,1)S(1)}, bf16[1,2,512,512]{3,2,1,0:T(8,128)(2,1)}, u32[]{:S(2)}) copy-start(bf16[1,2,512,512]{3,2,1,0:T(8,128)(2,1)} %nw1.1) | copy-start | bytes 3145732
  4.5 1.0 %copy-start.2 = (bf16[2,256,512]{2,1,0:T(8,128)(2,1)S(1)}, bf16[2,256,512]{2,1,0:T(8,128)(2,1)}, u32[]{:S(2)}) copy-start(bf16[2,256,512]{2,1,0:T(8,128)(2,1)} %nf.1) | copy-start | bytes 1572868
  5.5 1.0 %copy-start.3 = (bf16[1,512,512]{2,1,0:T(8,128)(2,1)S(1)}, bf16[1,512,512]{2,1,0:T(8,128)(2,1)}, u32[]{:S(2)}) copy-start(bf16[1,512,512]{2,1,0:T(8,128)(2,1)} %ew2.1) | copy-start | bytes 1572868
  6.6 1.0 %copy-start.4 = (bf16[1,512,512]{2,1,0:T(8,128)(2,1)S(1)}, bf16[1,512,512]{2,1,0:T(8,128)(2,1)}, u32[]{:S(2)}) copy-start(bf16[1,512,512]{2,1,0:T(8,128)(2,1)} %nw2.1) | copy-start | bytes 1572868
  7.6 0.7 %copy-start.5 = (s32[512]{0:T(512)S(1)}, s32[512]{0:T(512)}, u32[]{:S(2)}) copy-start(s32[512]{0:T(512)} %param.16) | copy-start | bytes 6148
  8.3 0.7 %copy-start.6 = (s32[512]{0:T(512)S(1)}, s32[512]{0:T(512)}, u32[]{:S(2)}) copy-start(s32[512]{0:T(512)} %param.17) | copy-start | bytes 6148
  9.0 0.7 %copy-start.7 = (bf16[1,512]{1,0:T(2,128)(2,1)S(1)}, bf16[1,512]{1,0:T(2,128)(2,1)}, u32[]{:S(2)}) copy-start(bf16[1,512]{1,0:T(2,128)(2,1)} %eb1.1) | copy-start | bytes 3076
  9.7 0.7 %copy-start.8 = (bf16[1,512]{1,0:T(2,128)(2,1)S(1)}, bf16[1,512]{1,0:T(2,128)(2,1)}, u32[]{:S(2)}) copy-start(bf16[1,512]{1,0:T(2,128)(2,1)} %eg.1) | copy-start | bytes 3076
  10.3 0.7 %copy-start.9 = (bf16[1,512]{1,0:T(2,128)(2,1)S(1)}, bf16[1,512]{1,0:T(2,128)(2,1)}, u32[]{:S(2)}) copy-start(bf16[1,512]{1,0:T(2,128)(2,1)} %nb1.1) | copy-start | bytes 3076
  11.0 0.7 %copy-start.10 = (bf16[1,512]{1,0:T(2,128)(2,1)S(1)}, bf16[1,512]{1,0:T(2,128)(2,1)}, u32[]{:S(2)}) copy-start(bf16[1,512]{1,0:T(2,128)(2,1)} %ng.1) | copy-start | bytes 3076

commit v2 on v1

--- a/solution.py
+++ b/solution.py
@@ -43,10 +43,10 @@
 
 
 def kernel(peers, hcap, chunks,
-           cnt, src, dst, send, eb1, eg, nb1, ng,
+           cnt_in, src_in, dst_in, send_in, eb1_in, eg_in, nb1_in, ng_in,
            nf, ef, ew1, ew2, nw1, nw2,
            no, eo,
-           nl, el, onl, oel, rhs, w1r, w2, n1, n2, msg, ohs, ohr, ohrt,
+           cnt, src, dst, send, eb1, eg, nb1, ng, nl, el, onl, oel, rhs, w1r, w2, n1, n2, msg, ohs, ohr, ohrt,
            out0, out1, halo, hx,
            wsem, lsem, hsem, osem, s0sem, s1sem, ssem):
     batches, nodes, width = nl.shape
@@ -62,16 +62,6 @@
 
     def peer(step):
         return lax.rem(me + step, peers)
-
-    @pl.loop(0, peers)
-    def _(step):
-        hail(1 - sec, peer(step))
-
-    @pl.when(sec == 0)
-    def _():
-        @pl.loop(1, peers)
-        def _(step):
-            hail(0, peer(step))
 
     at_e, at_r, at_s = nodes, nodes + width, 2 * nodes + width
 
@@ -88,6 +78,10 @@
         load(6, nw2.at[0], n2),
     ]
 
+    small = [load(7 + i, source, target) for i, (source, target) in enumerate([
+        (send_in, send), (src_in, src), (dst_in, dst), (cnt_in, cnt),
+        (eb1_in, eb1), (eg_in, eg), (nb1_in, nb1), (ng_in, ng)])]
+
     def node_in(m):
         return pltpu.make_async_copy(nf.at[m], nl.at[m], lsem.at[m, 0])
 
@@ -96,13 +90,25 @@
         return pltpu.make_async_copy(ef.at[m, pl.ds(lo, hi - lo)], el.at[m, pl.ds(lo, hi - lo)],
                                      lsem.at[m, 1 + c])
 
+    small[0].start()
+
     @pl.when(sec == 0)
     def _():
         for m in range(batches):
             node_in(m).start()
 
-    for copy in weights[:3]:
+    for copy in small[1:3] + weights[:3] + small[3:]:
         copy.start()
+
+    @pl.loop(0, peers)
+    def _(step):
+        hail(1 - sec, peer(step))
+
+    @pl.when(sec == 0)
+    def _():
+        @pl.loop(1, peers)
+        def _(step):
+            hail(0, peer(step))
 
     @pl.when(sec == 0)
     def _():
@@ -118,9 +124,9 @@
             for c in range(len(chunks)):
                 edge_in(m, c).start()
 
+    small[0].wait()
     send_hot = jnp.concatenate(
-        [(lax.broadcasted_iota(jnp.int32, (peers, nodes), 1) == send[:, k:k + 1]).astype(F32)
-         for k in range(hcap)], axis=0).astype(BF16)
+        [onehot(column(send[k:k + 1]), nodes) for k in range(hcap)], axis=0)
 
     def gather_rows(values, store):
         rows = dot(send_hot, values)
@@ -152,6 +158,8 @@
     def _():
         pl.semaphore_wait(barrier, peers)
 
+    for copy in small[1:]:
+        copy.wait()
     col_s = column(src[...])
     col_r = column(dst[...])
     ohs[...] = onehot(col_s, nodes)
@@ -163,7 +171,7 @@
     gain_e = eg[...].astype(F32)
     bias_n = nb1[...].astype(F32)
     gain_n = ng[...].astype(F32)
-    live = cnt[0]
+    live = cnt[...]
 
     def to_next(m, slot, source, target):
         return pltpu.make_async_remote_copy(
@@ -295,7 +303,6 @@
         chunks.append((start, min(edges, (start // BLOCK + 1) * BLOCK)))
     slots = len(chunks) + 1
     anywhere = pl.BlockSpec(memory_space=pl.ANY)
-    vmem = pl.BlockSpec(memory_space=pltpu.VMEM)
     dma = pltpu.SemaphoreType.DMA
     flops = 2 * batches * width * inner * (3 * edges + 6 * nodes)
     moved = 2 * (2 * batches * (nodes + edges) * width + 7 * width * inner)
@@ -303,9 +310,17 @@
         functools.partial(kernel, peers, hcap, chunks),
         out_shape=(jax.ShapeDtypeStruct((1, batches, nodes, width), BF16),
                    jax.ShapeDtypeStruct((1, batches, edges, width), BF16)),
-        in_specs=[pl.BlockSpec(memory_space=pltpu.SMEM)] + [vmem] * 7 + [anywhere] * 6,
+        in_specs=[anywhere] * 14,
         out_specs=(anywhere, anywhere),
         scratch_shapes=[
+            pltpu.VMEM((1, 1), jnp.int32),
+            pltpu.VMEM((1, edges), jnp.int32),
+            pltpu.VMEM((1, edges), jnp.int32),
+            pltpu.VMEM((hcap, peers), jnp.int32),
+            pltpu.VMEM((1, inner), BF16),
+            pltpu.VMEM((1, width), BF16),
+            pltpu.VMEM((1, inner), BF16),
+            pltpu.VMEM((1, width), BF16),
             pltpu.VMEM((batches, nodes, width), BF16),
             pltpu.VMEM((batches, edges, width), BF16),
             pltpu.VMEM((batches, nodes, width), BF16),
@@ -323,7 +338,7 @@
             pltpu.VMEM((batches, peers, hcap, width), F32),
             pltpu.VMEM((peers, batches, hcap, width), F32),
             pltpu.VMEM((halo_rows, width), F32),
-            dma((7,)),
+            dma((15,)),
             dma((batches, slots)),
             dma((batches,)),
             dma((batches, slots)),
@@ -332,9 +347,9 @@
             dma((batches, slots)),
         ],
         compiler_params=pltpu.CompilerParams(
-            collective_id=0, has_side_effects=True, vmem_limit_bytes=48 * 1024 * 1024),
+            collective_id=0, has_side_effects=True, vmem_limit_bytes=64 * 1024 * 1024),
         cost_estimate=pl.CostEstimate(flops=flops, bytes_accessed=moved, transcendentals=0),
-    )(edge_count, edge_src.reshape(1, -1), edge_dst.reshape(1, -1), send_rows,
+    )(edge_count.reshape(1, 1), edge_src.reshape(1, -1), edge_dst.reshape(1, -1), send_rows.T,
       edge_b1, edge_gain, node_b1, node_gain,
       node_feats, edge_feats, edge_w1, edge_w2, node_w1, node_w2)
 

time: 38.9 us -> 29.8 us (0.77)
  local copies, waits for them, and re-layouts: 12.2 us -> 2.93 us
  Pallas kernels: 24.9 us -> 25.4 us
    unnamed x25 -> x4, local copies, waits for them, and re-layouts: 12.2 us -> 2.93 us
    pallas_call x1, Pallas kernels: 24.9 us -> 25.4 us  [local(): pl.pallas_call(functools.partial(kernel, peers, hcap, chunks), out_shape=...]
where the time goes in v2:
time: 29.8 us; the launch traced here: 29.7 us
  Pallas kernels  25.4 us (85%)
  local copies, waits for them, and re-layouts  2.93 us (10%)
  between operations  1.3 us (4%)
    pallas_call x1, Pallas kernels, local(): pl.pallas_call(functools.partial(kernel, peers, hcap, chunks), out_shape=...  25.4 us
    unnamed x4, local copies, waits for them, and re-layouts  2.93 us

profile of v2, /device:TPU:1, one launch (start us, length us, event | category | flops | bytes accessed | tf_op | source)
XLA Modules:
  0.0 29.7 jit_solution(4718603032676990884)
XLA Ops:
  1.3 25.4 %shard_map.149 = (bf16[1,2,256,512]{3,2,1,0:T(8,128)(2,1)}, bf16[1,2,512,512]{3,2,1,0:T(8,128)(2,1)}) custom-call(s32[1,1]{1,0:T(1,128)} %bitcast.4.cnt_in, s32[1,512]{1,0:T(1,128)} %bitcast.5, s32[1,512]{1,0:T(1,128)} %bitcast.6, s32[2,16]{1,0:T(2,128)} %bitcast.7, bf16[1,512]{1,0:T(2,128)(2,1)} %eb1_in.1, bf16[1,512]{1,0:T(2,128)(2,1)} %eg_in.1, ...), custom_call_target="tpu_custom_call" | custom-call | flops 3221225472 | bytes 6815744 | tf_op jit(solution)/shard_map/pallas_call | solution.py:309
  26.7 0.0 copy-start
  26.7 2.0 %copy.19 = bf16[1,2,256,512]{3,2,1,0:T(8,128)(2,1)} copy(bf16[1,2,256,512]{3,2,1,0:T(8,128)(2,1)} %get-tuple-element.4) | data formatting | bytes 1048576
  28.7 0.0 copy-done
  28.7 1.0 %copy.20 = bf16[1,2,512,512]{3,2,1,0:T(8,128)(2,1)} copy(bf16[1,2,512,512]{3,2,1,0:T(8,128)(2,1)S(1)} %copy-done) | data formatting | bytes 2097152
Async XLA Ops:
  26.7 2.0 %copy-start = (bf16[1,2,512,512]{3,2,1,0:T(8,128)(2,1)S(1)}, bf16[1,2,512,512]{3,2,1,0:T(8,128)(2,1)}, u32[]{:S(2)}) copy-start(bf16[1,2,512,512]{3,2,1,0:T(8,128)(2,1)} %get-tuple-element.5) | copy-start | bytes 3145732
